TPU v7x, 512 devices: a whole 4x4x16 slice. The times are simulated.
512 devices in a mesh: row: 16 (over y, x_lo, core), col: 32 (over z, x_hi).
Axes of the slice: x: 4 (x_hi: 2, x_lo: 2; x = x_hi * 2 + x_lo), y: 4, z: 16, core: 2. Of those that a mesh axis runs over, the one named last changes fastest.
Arguments:
- features: bfloat16 [65536, 128], P(('row', 'col')), may hold values from -6 to 6
- weight: bfloat16 [128, 128], replicated, may hold values from -0.5 to 0.5
- bias: float32 [128], replicated, may hold values from -3 to 3
- tile_values: bfloat16 [16, 32, 38, 128, 128], P('row', 'col'), may hold values from -0.15625 to 0.15625
- tile_rows: int32 [16, 32, 38], P('row', 'col'), may hold values from 0 to 31
- tile_cols: int32 [16, 32, 38], P('row', 'col'), may hold values from 0 to 15
- tile_counts: int32 [16, 32], P('row', 'col'), may hold values from 4 to 38, as said below
- out_grad: bfloat16 [65536, 128], P(('row', 'col')), may hold values from -6 to 6
Outputs:
- activated: bfloat16 [65536, 128], P(('row', 'col'))
- x_grad: bfloat16 [65536, 128], P(('row', 'col'))
- weight_grad: float32 [128, 128], replicated
- bias_grad: float32 [128], replicated
Inputs may be any that keep to these rules, and one draw needn't show every extreme that they name: `tile_counts`: some grid cell has exactly 38 live slots in every draw.
All inputs are finite; a program needn't handle non-finite values.
Results may differ from a plain program's by a relative error of at most 0.024.
Values may be sent and summed in bfloat16 or wider, within the bound.
A program may use at most 64 MiB of HBM per device.

v0:
```python
import jax
import jax.numpy as jnp
from jax import lax
from jax.sharding import PartitionSpec as P


def silu_slope(value):
    sig = jax.nn.sigmoid(value)
    return sig * (1.0 + value * (1.0 - sig))


def aggregate(tiles, src_index, dst_index, count, source, n_out, flipped):
    height = source.shape[1]
    side = tiles.shape[1]
    source_blocks = source.reshape(-1, side, height)
    total_slots = tiles.shape[0]
    form = "tji,tjf->tif" if flipped else "tij,tjf->tif"
    targets = jnp.arange(n_out, dtype=jnp.int32)
    slot_ids = jnp.arange(total_slots, dtype=jnp.int32)
    picked = jnp.take(source_blocks, src_index, axis=0)
    prod = jnp.einsum(form, tiles, picked, preferred_element_type=jnp.float32)
    select = ((dst_index[None, :] == targets[:, None]) & (slot_ids[None, :] < count)).astype(
        jnp.bfloat16
    )
    high_part = lax.optimization_barrier(prod.astype(jnp.bfloat16))
    low_part = (prod - high_part.astype(jnp.float32)).astype(jnp.bfloat16)
    routed = jnp.einsum("bt,tif->bif", select, high_part, preferred_element_type=jnp.float32)
    summed = routed + jnp.einsum(
        "bt,tif->bif", select, low_part, preferred_element_type=jnp.float32
    )
    return summed.reshape(n_out * side, height)


def on_device(features, weight, bias, tile_values, tile_rows, tile_cols, tile_counts, out_grad):
    tiles = tile_values[0, 0]
    rows_list = tile_rows[0, 0]
    cols_list = tile_cols[0, 0]
    count = tile_counts[0, 0]
    slice_rows = features.shape[0]
    side = tiles.shape[1]
    row_blocks = lax.axis_size("col") * slice_rows // side
    panel_blocks = lax.axis_size("row") * slice_rows // side
    proj = jnp.dot(features, weight, preferred_element_type=jnp.float32).astype(jnp.bfloat16)
    panel = lax.all_gather(proj, "row", axis=0, tiled=True)
    partial_rows = aggregate(tiles, cols_list, rows_list, count, panel, row_blocks, False)
    pre = (
        lax.psum_scatter(
            partial_rows.astype(jnp.bfloat16), "col", scatter_dimension=0, tiled=True
        ).astype(jnp.float32)
        + bias[None, :]
    )
    grad_share = (out_grad.astype(jnp.float32) * silu_slope(pre)).astype(jnp.bfloat16)
    grad_rows = lax.all_gather(grad_share, "col", axis=0, tiled=True)
    activated = jax.nn.silu(pre).astype(jnp.bfloat16)
    partial_panel = aggregate(tiles, rows_list, cols_list, count, grad_rows, panel_blocks, True)
    back = lax.psum_scatter(
        partial_panel.astype(jnp.bfloat16), "row", scatter_dimension=0, tiled=True
    )
    x_grad = lax.dot_general(
        back, weight, (((1,), (1,)), ((), ())), preferred_element_type=jnp.float32
    ).astype(jnp.bfloat16)
    local_weight = lax.dot_general(
        features, back, (((0,), (0,)), ((), ())), preferred_element_type=jnp.float32
    )
    local_bias = jnp.sum(grad_share.astype(jnp.float32), axis=0)
    weight_grad, bias_grad = lax.psum((local_weight, local_bias), ("row", "col"))
    return (activated, x_grad, weight_grad, bias_grad)


def solution(mesh):
    return jax.shard_map(
        on_device,
        mesh=mesh,
        in_specs=(
            P(("row", "col"), None),
            P(),
            P(),
            P("row", "col", None, None, None),
            P("row", "col", None),
            P("row", "col", None),
            P("row", "col"),
            P(("row", "col"), None),
        ),
        out_specs=(P(("row", "col"), None), P(("row", "col"), None), P(), P()),
        check_vma=False,
    )
```

profile of v0, /device:TPU:1, one launch (start us, length us, event | category | flops | bytes accessed | tf_op | source)
XLA Modules:
  0.0 1397.8 jit_solution(14576645808126590213)
XLA Ops:
  7.2 0.0 copy-start
  7.2 0.0 reduce-scatter.3.cloned.1.call-start
  7.2 0.8 compare_and_fusion.1
  8.0 0.7 fusion.31
  9.3 0.9 convolution_convert_fusion.1
  10.2 25.7 %all_gather.6 = bf16[2048,128]{1,0:T(8,128)(2,1)S(1)} all-gather(bf16[128,128]{1,0:T(8,128)(2,1)S(1)} %convolution_convert_fusion.1), channel_id=1, replica_groups=mesh['row'=16,'col'=32] {'row'}, dimensions={0}, use_global_device_ids=true | all-gather | bytes 557056 | tf_op jit(solution)/shard_map/all_gather | solution.py:44
  35.9 1.9 gather_fusion
  37.8 0.0 copy-done
  37.8 3.9 bitcast_convert_fusion.1
  41.7 2.0 copy.18
  43.6 3.1 fusion.1
  46.8 2.8 copy.19
  49.6 0.0 copy-done.1
  49.6 0.0 copy-done.8
  49.6 0.4 fusion.16
  50.0 0.9 copy-done.2
  50.9 0.5 add_convert_fusion
  51.4 0.0 copy-start.7
  51.4 0.0 copy-start.10
  51.4 1.4 copy.20
  52.8 0.0 reduce-scatter.3.cloned.1.call-update
  52.8 0.0 all-gather.2.cloned.1.call-start
  52.9 628.7 %reduce-scatter.3.cloned.1.call-done = bf16[128,128]{1,0:T(8,128)(2,1)} async-done(((bf16[4096,128]{1,0:T(8,128)(2,1)}), bf16[128,128]{1,0:T(8,128)(2,1)}) %reduce-scatter.3.cloned.1.call-update) | async-done | bytes 32784 | tf_op jit(solution)/shard_map/reduce_scatter | solution.py:47
  681.6 0.0 copy-done.7
  681.6 1.4 convert_reduce_fusion
  683.0 0.0 all-gather.2.cloned.1.call-update
  683.0 0.0 reduce-scatter.5.cloned.1.call-start
  683.1 145.1 %all-gather.2.cloned.1.call-done = bf16[4096,128]{1,0:T(8,128)(2,1)} async-done(((bf16[128,128]{1,0:T(8,128)(2,1)}), bf16[4096,128]{1,0:T(8,128)(2,1)}) %all-gather.2.cloned.1.call-update) | async-done | bytes 1048592 | tf_op jit(solution)/shard_map/all_gather | solution.py:53
  828.2 3.1 gather_fusion.1
  831.3 3.4 bitcast_convert_fusion
  834.7 2.0 copy.22
  836.7 3.1 fusion
  839.8 2.8 copy.23
  842.6 0.0 copy-done.3
  842.6 0.4 fusion.25
  843.0 1.0 copy-done.4
  843.9 0.4 fusion.2
  844.3 0.0 copy-start.6
  844.3 0.0 copy-start.5
  844.3 0.9 copy.24
  845.3 0.0 reduce-scatter.5.cloned.1.call-update
  845.3 0.0 all-reduce.2.cloned.1.call-start
  845.3 109.7 %psum.15 = f32[128]{0:T(128)} all-reduce(f32[128]{0:T(128)S(1)} %get-tuple-element.12), channel_id=1, replica_groups=mesh['row'=16,'col'=32] {'row','col'}, use_global_device_ids=true, to_apply=%region_4.5 | all-reduce | flops 128 | bytes 1024 | tf_op jit(solution)/shard_map/psum | solution.py:66
  955.1 1.6 convolution_bitcast_fusion
  956.6 0.0 all-reduce.2.cloned.1.call-update
  956.7 1.5 convolution_convert_fusion
  958.2 431.5 %all-reduce.2.cloned.1.call-done = f32[128,128]{0,1:T(8,128)} async-done(((f32[128,128]{0,1:T(8,128)}), f32[128,128]{0,1:T(8,128)}) %all-reduce.2.cloned.1.call-update) | async-done | bytes 65552 | tf_op jit(solution)/shard_map/psum | solution.py:66
  1389.7 1.6 copy.25
  (16 shorter events, 0.0 us)
Async XLA Ops:
  7.2 30.6 %copy-start = (bf16[1,1,38,128,128]{4,3,2,1,0:T(8,128)(2,1)S(1)}, bf16[1,1,38,128,128]{4,3,2,1,0:T(8,128)(2,1)}, u32[]{:S(2)}) copy-start(bf16[1,1,38,128,128]{4,3,2,1,0:T(8,128)(2,1)} %param.11) | copy-start | bytes 3735556
  7.2 674.4 %reduce-scatter.3.cloned.1.call-start = ((), (), s32[]{:S(2)}) async-start(), calls=%async_computation.2 | async-start | bytes 1081344 | tf_op jit(solution)/shard_map/reduce_scatter | solution.py:47
  46.8 2.8 copy-start.1
  46.8 2.8 copy-start.8
  49.6 1.3 copy-start.2
  51.4 630.2 %copy-start.7 = (bf16[128,128]{1,0:T(8,128)(2,1)S(1)}, bf16[128,128]{1,0:T(8,128)(2,1)}, u32[]{:S(2)}) copy-start(bf16[128,128]{1,0:T(8,128)(2,1)} %param.15) | copy-start | bytes 98308
  51.4 630.2 %copy-start.10 = (f32[128]{0:T(128)S(1)}, f32[128]{0:T(128)}, u32[]{:S(2)}) copy-start(f32[128]{0:T(128)} %param.10) | copy-start | bytes 1540
  52.8 775.4 %all-gather.2.cloned.1.call-start = ((), (), s32[]{:S(2)}) async-start(), calls=%async_computation.3 | async-start | bytes 1081344 | tf_op jit(solution)/shard_map/all_gather | solution.py:53
  683.0 272.0 %reduce-scatter.5.cloned.1.call-start = ((), (), s32[]{:S(2)}) async-start(), calls=%async_computation.4 | async-start | bytes 557056 | tf_op jit(solution)/shard_map/reduce_scatter | solution.py:56
  839.8 2.8 copy-start.3
  839.8 2.8 copy-start.9
  842.6 1.3 copy-start.4
  844.3 110.7 %copy-start.6 = (bf16[128,128]{1,0:T(8,128)(2,1)S(1)}, bf16[128,128]{1,0:T(8,128)(2,1)}, u32[]{:S(2)}) copy-start(bf16[128,128]{1,0:T(8,128)(2,1)} %param.8) | copy-start | bytes 98308
  844.3 112.3 %copy-start.5 = (bf16[128,128]{1,0:T(8,128)(2,1)S(1)}, bf16[128,128]{1,0:T(8,128)(2,1)}, u32[]{:S(2)}) copy-start(bf16[128,128]{1,0:T(8,128)(2,1)} %param.9) | copy-start | bytes 98308
  845.3 544.4 %all-reduce.2.cloned.1.call-start = ((), (), s32[]{:S(2)}) async-start(), calls=%async_computation.5 | async-start | bytes 131072 | tf_op jit(solution)/shard_map/psum | solution.py:66
Sparse Core Ops, SparseCore 0:
  52.9 628.5 reduce-scatter.2
  685.7 142.4 all-gather.1
  845.4 69.2 reduce-scatter.4
  956.8 432.9 all-reduce.1
where the time goes:
time: 1400 us
  waiting for transfers between devices  1210 us (86%)
  blocking collectives  135 us (10%)
  local copies, waits for them, and re-layouts  20.3 us (1%)
  between operations  14.5 us (1%)
    reduce_scatter x1, waiting for transfers between devices, on_device(): lax.psum_scatter(partial_rows.astype(jnp.bfloat16), 'col', scatter_dimens...  629 us
    psum x1, waiting for transfers between devices, on_device(): lax.psum((local_weight, local_bias), ('row', 'col'))  432 us
    all_gather x1, waiting for transfers between devices, on_device(): grad_rows = lax.all_gather(grad_share, 'col', axis=0, tiled=True)  145 us
    psum x1, blocking collectives, on_device(): lax.psum((local_weight, local_bias), ('row', 'col'))  110 us
  transfers between devices with their start and end apart: 4, of which 3 were waited for; matrix products, arithmetic and copies ran while one was open for 0% of the time, Pallas kernels for 0%

commit v1 on v0

v1 whole, which is shorter than its diff:
```python
import jax
import jax.numpy as jnp
from jax import lax
from jax.experimental import pallas as pl
from jax.experimental.pallas import tpu as pltpu
from jax.sharding import PartitionSpec as P

MESH = pl.DeviceIdType.MESH
F32 = jnp.float32
BF16 = jnp.bfloat16
SIDE = 128
SLOTS = 38
NY, NZ, NCORE = 4, 16, 2
N_ROW, N_COL = 16, 32

CHIPS = ((2, 1), (2, 0), (1, 1), (3, 1), (1, 0), (3, 0), (0, 1))
PARENT = {2: 0, 6: 0, -2: 0, -6: 0, 1: 2, 3: 2, 4: 2, 5: 6, 7: 6, 8: 6, -1: -2, -3: -2, -4: -2, -5: -6, -7: -6}
CHILDREN = {p: [q for q in PARENT if PARENT[q] == p] for p in (0, 2, -2, 6, -6)}
REDUCE_ORDER = (8, 7, 5, -7, -5, 4, -4, 6, -6, 3, -3, 1, -1, 2, -2, 0)
GATHER_ORDER = (2, -2, 6, -6, 1, -1, 3, -3, 4, -4, 5, -5, 7, -7, 8)
ROUND_A = ((4, 0), (12, 0), (8, 0))
ROUND_B = ((0, 1), (1, 0), (15, 0), (2, 0), (1, 1), (15, 1), (2, 1))
ROW_PEERS = tuple((dy, dx, dk) for dy in range(4) for dx in range(2) for dk in range(2) if (dy, dx, dk) != (0, 0, 0))


def kernel(
    feat, weight, bias, tiles_hbm, rows, cols, counts, out_grad,
    act_out, xg_out, wg_out, bg_out,
    tiles, panel, partial, grads, table, tab,
    xs, xr, zs, zr, cs, cr, hs, hr, ws, wr, acc_a, wra, acc_b, wrb, fin,
    sem, p_s, p_r, f_s, f_r, xs_s, xs_r, zs_s, zs_r, g_s, g_r, gx_s, gx_r,
    c_s, c_r, h_s, h_r, w_s, w_r, a_s, a_r, b_s, b_r, e_s, e_r,
):
    r = lax.axis_index("row")
    c = lax.axis_index("col")
    core, xl, y = r % 2, (r // 2) % 2, r // 4
    z, xh = c // 2, c % 2

    def in_row(dy, dx, dk):
        xx = xl + dx - 2 * xl * dx
        kk = core + dk - 2 * core * dk
        return ((y + dy) % NY) * 4 + xx * 2 + kk

    def in_col(dz, dh):
        hh = xh + dh - 2 * xh * dh
        return ((z + dz + NZ) % NZ) * 2 + hh

    def send(src, dst, ss, rs, row, col):
        copy = pltpu.make_async_remote_copy(
            src_ref=src, dst_ref=dst, send_sem=ss, recv_sem=rs, device_id=(row, col), device_id_type=MESH
        )
        copy.start()
        started.append(copy)

    def landed(dst, rs):
        pltpu.make_async_remote_copy(
            src_ref=dst, dst_ref=dst, send_sem=rs, recv_sem=rs, device_id=(r, c), device_id_type=MESH
        ).wait_recv()

    started = []
    fetch = pltpu.make_async_copy(tiles_hbm, tiles, sem.at[0])
    fetch.start()

    barrier = pltpu.get_barrier_semaphore()
    greet = [(in_row(0, 0, 1), c)] + [(in_row(dy, dx, 0), c) for dy, dx in CHIPS]
    greet += [(r, in_col(0, 1))] + [(r, in_col(d, 0)) for d in (1, -1, 2, -2, 6, -6)]
    for row, col in greet:
        pl.semaphore_signal(barrier, inc=1, device_id=(row, col), device_id_type=MESH)

    lane = lax.broadcasted_iota(jnp.int32, (SIDE, SIDE), 1)
    sub = lax.broadcasted_iota(jnp.int32, (SIDE, SIDE), 0)
    live = sub < counts[0, 0]
    for k, ref in ((0, rows), (1, cols)):
        padded = jnp.concatenate([ref[...], jnp.zeros((1, SIDE - SLOTS), jnp.int32)], axis=1)
        along = jnp.broadcast_to(padded, (SIDE, SIDE))
        down = jnp.sum(jnp.where(lane == sub, along, 0), axis=1, keepdims=True)
        down = jnp.broadcast_to(down, (SIDE, SIDE))
        prev = jnp.max(jnp.where((down == along) & (sub < lane) & live, sub + 1, 0), axis=0, keepdims=True)
        last = jnp.max(jnp.where((down == lane) & live, sub + 1, 0), axis=0, keepdims=True)
        table[k : k + 1, :] = padded
        table[2 + k : 3 + k, :] = prev
        table[4 + k : 5 + k, :] = last
    table[6:8, :] = jnp.zeros((2, SIDE), jnp.int32)
    to_scalar = pltpu.make_async_copy(table, tab, sem.at[1])
    to_scalar.start()
    panel[r] = feat[...]
    partial[0] = jnp.zeros((SIDE, SIDE), F32)

    pl.semaphore_wait(barrier, len(greet))

    for k, (dy, dx) in enumerate(CHIPS):
        send(feat, panel.at[r], p_s.at[k], p_r.at[k], in_row(dy, dx, 0), c)
    send(feat, panel.at[r], p_s.at[7], p_r.at[7], in_row(0, 0, 1), c)
    for k in (6, 4, 5, 1, 2, 3, 0):
        dy, dx = CHIPS[k]
        p = in_row(4 - dy, dx, 0)
        landed(panel.at[p], p_r.at[k])
        send(panel.at[p], panel.at[p], f_s.at[k], f_r.at[k], in_row(0, 0, 1), c)
    landed(panel.at[in_row(0, 0, 1)], p_r.at[7])
    to_scalar.wait()
    fetch.wait()
    for k, (dy, dx) in enumerate(CHIPS):
        landed(panel.at[in_row(4 - dy, dx, 1)], f_r.at[k])

    def forward(t, carry):
        prod = jnp.dot(tiles[t], panel[tab[1, t]], preferred_element_type=F32)
        partial[t + 1] = prod + partial[tab[2, t]]
        return carry

    lax.fori_loop(0, SLOTS, forward, 0, unroll=True)

    for e in REDUCE_ORDER:
        b = in_col(-e, 1)
        xs[e % NZ] = partial[tab[4, b]].astype(BF16)
        send(xs.at[e % NZ], xr.at[e % NZ], xs_s.at[e % NZ], xs_r.at[e % NZ], r, in_col(0, 1))
    total = None
    for e in REDUCE_ORDER:
        i = e % NZ
        total = partial[tab[4, in_col(-e, 0)]]
        for q in CHILDREN.get(e, ()):
            landed(zr.at[q % NZ], zs_r.at[q % NZ])
            total += zr[q % NZ].astype(F32)
        landed(xr.at[i], xs_r.at[i])
        total += xr[i].astype(F32)
        if e != 0:
            zs[i] = total.astype(BF16)
            send(zs.at[i], zr.at[i], zs_s.at[i], zs_r.at[i], r, in_col(PARENT[e] - e, 0))

    agg = total.astype(BF16)
    pre = jnp.dot(agg, weight[...], preferred_element_type=F32) + bias[...]
    sig = 1.0 / (1.0 + jnp.exp(-pre))
    grad = (out_grad[...].astype(F32) * (sig * (1.0 + pre * (1.0 - sig)))).astype(BF16)
    grads[c] = grad.T

    for k in (6, -6):
        send(grads.at[c], grads.at[c], g_s.at[k % NZ], g_r.at[k % NZ], r, in_col(k, 0))
    send(grads.at[c], grads.at[c], gx_s.at[0], gx_r.at[0], r, in_col(0, 1))
    for k in (2, -2):
        send(grads.at[c], grads.at[c], g_s.at[k % NZ], g_r.at[k % NZ], r, in_col(k, 0))

    act_out[...] = (pre * sig).astype(BF16)
    wgrad = lax.dot_general(agg, grad, (((0,), (0,)), ((), ())), preferred_element_type=F32)
    bgrad = jnp.sum(grad.astype(F32).reshape(16, 8, SIDE), axis=0)
    ws[:, 0:8, :] = wgrad.reshape(N_ROW, 8, SIDE)
    ws[:, 8:16, :] = jnp.broadcast_to(bgrad[None], (N_ROW, 8, SIDE))
    for k, (dy, dx, dk) in enumerate(ROW_PEERS):
        to = in_row(dy, dx, dk)
        send(ws.at[to], wr.at[k], w_s.at[k], w_r.at[k], to, c)

    def take(d):
        i = d % NZ
        b = in_col(-d, 0)
        landed(grads.at[b], g_r.at[i])
        for q in CHILDREN.get(d, ()):
            send(grads.at[b], grads.at[b], g_s.at[q % NZ], g_r.at[q % NZ], r, in_col(q - d, 0))
        send(grads.at[b], grads.at[b], gx_s.at[i], gx_r.at[i], r, in_col(0, 1))

    for d in GATHER_ORDER[:4]:
        take(d)
    total = ws[r]
    for k in range(len(ROW_PEERS)):
        landed(wr.at[k], w_r.at[k])
        total += wr[k]
    acc_a[...] = total
    for k, (dz, dh) in enumerate(ROUND_A):
        send(acc_a, wra.at[k], a_s.at[k], a_r.at[k], r, in_col(dz, dh))
    for d in GATHER_ORDER[4:]:
        take(d)
    total = acc_a[...]
    for k in range(len(ROUND_A)):
        landed(wra.at[k], a_r.at[k])
        total += wra[k]
    acc_b[...] = total
    for k, (dz, dh) in enumerate(ROUND_B):
        send(acc_b, wrb.at[k], b_s.at[k], b_r.at[k], r, in_col(dz, dh))
    landed(grads.at[in_col(0, 1)], gx_r.at[0])
    for d in GATHER_ORDER:
        landed(grads.at[in_col(-d, 1)], gx_r.at[d % NZ])

    def backward(t, carry):
        prod = jnp.dot(grads[tab[0, t]], tiles[t], preferred_element_type=F32)
        partial[t + 1] = prod + partial[tab[3, t]]
        return carry

    lax.fori_loop(0, SLOTS, backward, 0, unroll=True)

    for k, (dy, dx) in enumerate(CHIPS + ((0, 0),)):
        cs[k] = partial[tab[5, in_row(dy, dx, 1)]].astype(BF16)
        send(cs.at[k], cr.at[k], c_s.at[k], c_r.at[k], in_row(0, 0, 1), c)
    for k, (dy, dx) in enumerate(CHIPS):
        landed(cr.at[k], c_r.at[k])
        hs[k] = (partial[tab[5, in_row(dy, dx, 0)]] + cr[k].astype(F32)).astype(BF16)
        send(hs.at[k], hr.at[k], h_s.at[k], h_r.at[k], in_row(dy, dx, 0), c)

    total = acc_b[...]
    for k in range(len(ROUND_B)):
        landed(wrb.at[k], b_r.at[k])
        total += wrb[k]
    fin[r] = total[0:8]
    bg_out[...] = jnp.sum(total[8:16], axis=0, keepdims=True)
    for k, (dy, dx, dk) in enumerate(ROW_PEERS):
        send(fin.at[r], fin.at[r], e_s.at[k], e_r.at[k], in_row(dy, dx, dk), c)

    landed(cr.at[7], c_r.at[7])
    total = partial[tab[5, r]] + cr[7].astype(F32)
    for k in (6, 4, 5, 1, 2, 3, 0):
        landed(hr.at[k], h_r.at[k])
        total += hr[k].astype(F32)
    back = total.astype(BF16)
    xg_out[...] = lax.dot_general(
        back, weight[...], (((0,), (1,)), ((), ())), preferred_element_type=F32
    ).astype(BF16)
    for k, (dy, dx, dk) in enumerate(ROW_PEERS):
        landed(fin.at[in_row(4 - dy, dx, dk)], e_r.at[k])
    wg_out[...] = fin[...].reshape(SIDE, SIDE)
    for copy in started:
        copy.wait_send()


def on_device(features, weight, bias, tile_values, tile_rows, tile_cols, tile_counts, out_grad):
    vmem = pl.BlockSpec(memory_space=pltpu.VMEM)
    dma = pltpu.SemaphoreType.DMA
    block = (SIDE, SIDE)
    act, xg, wg, bg = pl.pallas_call(
        kernel,
        name="gcn",
        out_shape=(
            jax.ShapeDtypeStruct(block, BF16),
            jax.ShapeDtypeStruct(block, BF16),
            jax.ShapeDtypeStruct(block, F32),
            jax.ShapeDtypeStruct((1, SIDE), F32),
        ),
        in_specs=[
            vmem, vmem, vmem, pl.BlockSpec(memory_space=pl.ANY), vmem, vmem,
            pl.BlockSpec(memory_space=pltpu.SMEM), vmem,
        ],
        out_specs=(vmem,) * 4,
        scratch_shapes=[
            pltpu.VMEM((SLOTS,) + block, BF16),
            pltpu.VMEM((N_ROW,) + block, BF16),
            pltpu.VMEM((SLOTS + 1,) + block, F32),
            pltpu.VMEM((N_COL,) + block, BF16),
            pltpu.VMEM((8, SIDE), jnp.int32),
            pltpu.SMEM((8, SIDE), jnp.int32),
            pltpu.VMEM((NZ,) + block, BF16),
            pltpu.VMEM((NZ,) + block, BF16),
            pltpu.VMEM((NZ,) + block, BF16),
            pltpu.VMEM((NZ,) + block, BF16),
            pltpu.VMEM((8,) + block, BF16),
            pltpu.VMEM((8,) + block, BF16),
            pltpu.VMEM((7,) + block, BF16),
            pltpu.VMEM((7,) + block, BF16),
            pltpu.VMEM((N_ROW, 16, SIDE), F32),
            pltpu.VMEM((15, 16, SIDE), F32),
            pltpu.VMEM((16, SIDE), F32),
            pltpu.VMEM((3, 16, SIDE), F32),
            pltpu.VMEM((16, SIDE), F32),
            pltpu.VMEM((7, 16, SIDE), F32),
            pltpu.VMEM((N_ROW, 8, SIDE), F32),
            dma((2,)),
            dma((8,)), dma((8,)), dma((7,)), dma((7,)),
            dma((NZ,)), dma((NZ,)), dma((NZ,)), dma((NZ,)),
            dma((NZ,)), dma((NZ,)), dma((NZ,)), dma((NZ,)),
            dma((8,)), dma((8,)), dma((7,)), dma((7,)),
            dma((15,)), dma((15,)), dma((3,)), dma((3,)), dma((7,)), dma((7,)), dma((15,)), dma((15,)),
        ],
        compiler_params=pltpu.CompilerParams(
            collective_id=0, has_side_effects=True, vmem_limit_bytes=32 << 20
        ),
    )(
        features, weight, bias.reshape(1, SIDE), tile_values[0, 0],
        tile_rows[0], tile_cols[0], tile_counts, out_grad,
    )
    return act, xg, wg, bg.reshape(SIDE)


def solution(mesh):
    return jax.shard_map(
        on_device,
        mesh=mesh,
        in_specs=(
            P(("row", "col"), None),
            P(),
            P(),
            P("row", "col", None, None, None),
            P("row", "col", None),
            P("row", "col", None),
            P("row", "col"),
            P(("row", "col"), None),
        ),
        out_specs=(P(("row", "col"), None), P(("row", "col"), None), P(), P()),
        check_vma=False,
    )
```

time: 1400 us -> 85.6 us (0.06)
  waiting for transfers between devices: 1210 us -> 0 us
  blocking collectives: 135 us -> 0 us
  Pallas kernels: 0 us -> 75.8 us
    reduce_scatter x2 -> x0, waiting for transfers between devices: 629 us -> none  [the longest x1 629 us: on_device(): lax.psum_scatter(partial_rows.astype(jnp.bfloat16), 'col', scatter_dimens...]
    psum x1 -> x0, waiting for transfers between devices: 432 us -> none  [on_device(): lax.psum((local_weight, local_bias), ('row', 'col'))]
    all_gather x1 -> x0, waiting for transfers between devices: 145 us -> none  [on_device(): grad_rows = lax.all_gather(grad_share, 'col', axis=0, tiled=True)]
    psum x1 -> x0, blocking collectives: 110 us -> none  [on_device(): lax.psum((local_weight, local_bias), ('row', 'col'))]
    pallas_call x0 -> x1, Pallas kernels: none -> 75.8 us  [on_device(): pl.pallas_call(kernel, name='gcn', out_shape=(jax.ShapeDtypeStruct(block,...]
    all_gather x1 -> x0, blocking collectives: 25.7 us -> none  [on_device(): panel = lax.all_gather(proj, 'row', axis=0, tiled=True)]
  transfers between devices with their start and end apart: 4 -> 0, of which waited for: 3 -> 0; matrix products, arithmetic and copies ran while one was open for 0% -> 0% of each run, Pallas kernels for 0% -> 0%
where the time goes in v1:
time: 85.6 us; the launch traced here: 85 us
  Pallas kernels  75.8 us (89%)
  local copies, waits for them, and re-layouts  7.89 us (9%)
  between operations  1.3 us (2%)
    pallas_call x1, Pallas kernels, on_device(): pl.pallas_call(kernel, name='gcn', out_shape=(jax.ShapeDtypeStruct(block,...  75.8 us
    unnamed x18, local copies, waits for them, and re-layouts  7.89 us

profile of v1, /device:TPU:1, one launch (start us, length us, event | category | flops | bytes accessed | tf_op | source)
XLA Modules:
  0.0 85.0 jit_solution(18410929395387256495)
XLA Ops:
  1.3 0.0 copy-start
  1.3 1.3 %copy-done = bf16[1,1,38,128,128]{4,3,2,1,0:T(8,128)(2,1)S(1)} copy-done((bf16[1,1,38,128,128]{4,3,2,1,0:T(8,128)(2,1)S(1)}, bf16[1,1,38,128,128]{4,3,2,1,0:T(8,128)(2,1)}, u32[]{:S(2)}) %copy-start) | copy-done | bytes 1245208
  2.6 0.0 copy-start.1
  2.6 0.8 copy-done.1
  3.3 0.0 copy-start.2
  3.3 0.8 copy-done.2
  4.1 0.0 copy-start.3
  4.1 0.8 copy-done.3
  4.8 0.0 copy-start.4
  4.9 0.7 copy-done.4
  5.5 0.0 copy-start.5
  5.5 0.7 copy-done.5
  6.2 0.0 copy-start.6
  6.2 0.7 copy-done.6
  6.8 75.8 %gcn.1 = (bf16[128,128]{1,0:T(8,128)(2,1)S(1)}, bf16[128,128]{1,0:T(8,128)(2,1)S(1)}, f32[128,128]{1,0:T(8,128)S(1)}, f32[1,128]{1,0:T(1,128)S(1)}) custom-call(bf16[128,128]{1,0:T(8,128)(2,1)S(1)} %copy-done.1, bf16[128,128]{1,0:T(8,128)(2,1)S(1)} %copy-done.2, f32[1,128]{1,0:T(1,128)S(1)} %bitcast.6, bf16[38,128,128]{2,1,0:T(8,128)(2,1)S(1)} %bitcast.5, ...), custom_call_target="tpu_custom_call" | custom-call | tf_op jit(solution)/shard_map/gcn/pallas_call | solution.py:224
  82.6 0.6 copy.17
  83.2 0.6 copy.18
  83.9 0.6 copy.19
  84.5 0.5 copy.20
Async XLA Ops:
  1.3 1.3 %copy-start = (bf16[1,1,38,128,128]{4,3,2,1,0:T(8,128)(2,1)S(1)}, bf16[1,1,38,128,128]{4,3,2,1,0:T(8,128)(2,1)}, u32[]{:S(2)}) copy-start(bf16[1,1,38,128,128]{4,3,2,1,0:T(8,128)(2,1)} %param.11) | copy-start | bytes 3735556
  2.6 0.8 copy-start.1
  3.3 0.8 copy-start.2
  4.1 0.8 copy-start.3
  4.8 0.7 copy-start.4
  5.5 0.7 copy-start.5
  6.2 0.7 copy-start.6

commit v2 on v1

v2 whole, which is shorter than its diff:
```python
import jax
import jax.numpy as jnp
from jax import lax
from jax.experimental import pallas as pl
from jax.experimental.pallas import tpu as pltpu
from jax.sharding import PartitionSpec as P

MESH = pl.DeviceIdType.MESH
F32 = jnp.float32
BF16 = jnp.bfloat16
SIDE = 128
SLOTS = 38
NY, NZ, NCORE = 4, 16, 2
N_ROW, N_COL = 16, 32

CHIPS = ((2, 1), (2, 0), (1, 1), (3, 1), (1, 0), (3, 0), (0, 1))
SUM_PARENT = {
    -7: -6, -6: -5, -5: 0, -4: -5, -3: -2, -2: 0, -1: 0, 1: 0, 2: 0, 3: 2, 4: 5, 5: 0, 6: 5, 7: 6, 8: 5,
}
SUM_BOTH = (-7, -6, -3, 3, 6, 7)
SUM_PLAN = (
    ("z2", 7), ("x", 8), ("z2", -7), ("z1", -7), ("x", -4), ("z2", -3), ("z1", 7), ("x", 4), ("x", 0), ("x", 1),
    ("z2", 3), ("x", -1), ("z1", -3), ("z1", 3), ("z2", 6), ("z2", -6), ("z1", 6), ("z1", -6), ("z1", 8), ("x", 2),
    ("x", -2), ("z1", -4), ("z1", 4), ("x", 5), ("x", -5), ("z1", 1), ("z1", -1), ("z1", 2), ("z1", -2), ("z1", 5),
    ("z1", -5),
)
GET_PARENT = {
    -7: -6, -6: 0, -5: -6, -4: -3, -3: -2, -2: 0, -1: -2, 1: 2, 2: 0, 3: 2, 4: 3, 5: 6, 6: 0, 7: 6, 8: 7,
}
GET_BOTH = (-7, -4, 1, 4, 7)
GET_CROSS = (-3, 3, 5, 8)
GET_FIRST = (("z1", 6), ("z1", -6), ("z1", 2), ("z1", -2), ("x", 0))
GET_NEXT = (
    ("dg", 3), ("z1", 3), ("x", 2), ("z1", 1), ("z1", -3), ("x", -2), ("dg", -3), ("z1", -1),
)
GET_LAST = (
    ("x", 6), ("z1", 7), ("dg", 5), ("z1", 5), ("z1", -7), ("x", -6), ("z1", -5), ("z2", 1), ("z1", 4), ("z1", -4),
    ("z2", 4), ("x", -1), ("dg", 8), ("z1", 8), ("z2", -4), ("x", -5), ("z2", 7), ("z2", -7),
)
ROUND_A = ((4, 0), (12, 0), (8, 0))
ROUND_B = ((0, 1), (1, 0), (15, 0), (2, 0), (1, 1), (15, 1), (2, 1))
ROW_PEERS = tuple((dy, dx, dk) for dy in range(4) for dx in range(2) for dk in range(2) if (dy, dx, dk) != (0, 0, 0))


def kernel(
    feat_hbm, weight_hbm, bias_hbm, tiles_hbm, rows_hbm, cols_hbm, counts_hbm, out_grad_hbm,
    act_out, back_out, wg_out, bg_out,
    weight, bias, rows, cols, counts, out_grad, tiles, panel, partial, grads, table, tab,
    xs, xr, z1s, z1r, z2s, z2r, cs, cr, hs, hr, ws, wr, acc_a, wra, acc_b, wrb, fin,
    sem, ring, p_s, p_r, f_s, f_r, xs_s, xs_r, z1_s, z1_r, z2_s, z2_r,
    g1_s, g1_r, g2_s, g2_r, gd_s, gd_r, gx_s, gx_r,
    c_s, c_r, h_s, h_r, w_s, w_r, a_s, a_r, b_s, b_r, e_s, e_r,
):
    r = lax.axis_index("row")
    c = lax.axis_index("col")
    core, xl, y = r % 2, (r // 2) % 2, r // 4
    z, xh = c // 2, c % 2

    def in_row(dy, dx, dk):
        xx = xl + dx - 2 * xl * dx
        kk = core + dk - 2 * core * dk
        return ((y + dy) % NY) * 4 + xx * 2 + kk

    def in_col(dz, dh):
        hh = xh + dh - 2 * xh * dh
        return ((z + dz + NZ) % NZ) * 2 + hh

    def send(src, dst, ss, rs, row, col):
        copy = pltpu.make_async_remote_copy(
            src_ref=src, dst_ref=dst, send_sem=ss, recv_sem=rs, device_id=(row, col), device_id_type=MESH
        )
        copy.start()
        started.append(copy)

    def landed(dst, rs):
        pltpu.make_async_remote_copy(
            src_ref=dst, dst_ref=dst, send_sem=rs, recv_sem=rs, device_id=(r, c), device_id_type=MESH
        ).wait_recv()

    started = []
    g_s = {"z1": g1_s, "z2": g2_s, "dg": gd_s, "x": gx_s}
    g_r = {"z1": g1_r, "z2": g2_r, "dg": gd_r, "x": gx_r}
    fetch = [
        pltpu.make_async_copy(src, dst, sem.at[k])
        for k, (src, dst) in enumerate(
            (
                (feat_hbm, panel.at[r]), (rows_hbm, rows), (cols_hbm, cols), (counts_hbm, counts),
                (tiles_hbm, tiles), (weight_hbm, weight), (bias_hbm, bias), (out_grad_hbm, out_grad),
            )
        )
    ]
    for copy in fetch:
        copy.start()

    barrier = pltpu.get_barrier_semaphore()
    greet = [(in_row(0, 0, 1), c)] + [(in_row(dy, dx, 0), c) for dy, dx in CHIPS]
    greet += [(r, in_col(0, 1))] + [(r, in_col(d, 0)) for d in (1, -1, 2, -2, 3, -3)]
    for row, col in greet:
        pl.semaphore_signal(barrier, inc=1, device_id=(row, col), device_id_type=MESH)

    for k in (1, 2, 3):
        fetch[k].wait()
    lane = lax.broadcasted_iota(jnp.int32, (SIDE, SIDE), 1)
    sub = lax.broadcasted_iota(jnp.int32, (SIDE, SIDE), 0)
    live = sub < counts[0, 0]
    for k, ref in ((0, rows), (1, cols)):
        padded = jnp.concatenate([ref[...], jnp.zeros((1, SIDE - SLOTS), jnp.int32)], axis=1)
        along = jnp.broadcast_to(padded, (SIDE, SIDE))
        down = jnp.sum(jnp.where(lane == sub, along, 0), axis=1, keepdims=True)
        down = jnp.broadcast_to(down, (SIDE, SIDE))
        prev = jnp.max(jnp.where((down == along) & (sub < lane) & live, sub + 1, 0), axis=0, keepdims=True)
        last = jnp.max(jnp.where((down == lane) & live, sub + 1, 0), axis=0, keepdims=True)
        table[k : k + 1, :] = padded
        table[2 + k : 3 + k, :] = prev
        table[4 + k : 5 + k, :] = last
    table[6:8, :] = jnp.zeros((2, SIDE), jnp.int32)
    to_scalar = pltpu.make_async_copy(table, tab, sem.at[8])
    to_scalar.start()
    partial[0] = jnp.zeros((SIDE, SIDE), F32)

    fetch[0].wait()
    pl.semaphore_wait(barrier, len(greet))

    for d in (3, -3):
        pl.semaphore_signal(ring, inc=1, device_id=(r, in_col(d, 0)), device_id_type=MESH)

    for k, (dy, dx) in enumerate(CHIPS):
        send(panel.at[r], panel.at[r], p_s.at[k], p_r.at[k], in_row(dy, dx, 0), c)
    send(panel.at[r], panel.at[r], p_s.at[7], p_r.at[7], in_row(0, 0, 1), c)
    for k in (6, 4, 5, 1, 2, 3, 0):
        dy, dx = CHIPS[k]
        p = in_row(4 - dy, dx, 0)
        landed(panel.at[p], p_r.at[k])
        send(panel.at[p], panel.at[p], f_s.at[k], f_r.at[k], in_row(0, 0, 1), c)
    landed(panel.at[in_row(0, 0, 1)], p_r.at[7])
    to_scalar.wait()
    fetch[4].wait()
    for k, (dy, dx) in enumerate(CHIPS):
        landed(panel.at[in_row(4 - dy, dx, 1)], f_r.at[k])

    def forward(t, carry):
        prod = jnp.dot(tiles[t], panel[tab[1, t]], preferred_element_type=F32)
        partial[t + 1] = prod + partial[tab[2, t]]
        return carry

    lax.fori_loop(0, SLOTS, forward, 0, unroll=True)

    pl.semaphore_wait(ring, 2)

    def collect(e, kind):
        i = e % NZ
        own = in_col(-e, 0) if kind == "z1" else in_col(-e, 1)
        value = partial[tab[4, own]]
        for q in SUM_PARENT:
            if SUM_PARENT[q] == e and (kind == "z1" or q in SUM_BOTH):
                buf, got = (z1r, z1_r) if kind == "z1" else (z2r, z2_r)
                landed(buf.at[q % NZ], got.at[q % NZ])
                value += buf[q % NZ].astype(F32)
        if kind == "z1" and e not in SUM_BOTH:
            landed(xr.at[i], xs_r.at[i])
            value += xr[i].astype(F32)
        return value

    for kind, e in SUM_PLAN:
        i = e % NZ
        value = collect(e, kind).astype(BF16)
        if kind == "x":
            xs[i] = value
            send(xs.at[i], xr.at[i], xs_s.at[i], xs_r.at[i], r, in_col(0, 1))
        elif kind == "z1":
            z1s[i] = value
            send(z1s.at[i], z1r.at[i], z1_s.at[i], z1_r.at[i], r, in_col(SUM_PARENT[e] - e, 0))
        else:
            z2s[i] = value
            send(z2s.at[i], z2r.at[i], z2_s.at[i], z2_r.at[i], r, in_col(SUM_PARENT[e] - e, 0))
    total = collect(0, "z1")

    for k in (5, 6, 7):
        fetch[k].wait()
    agg = total.astype(BF16)
    pre = jnp.dot(agg, weight[...], preferred_element_type=F32) + bias[...]
    sig = 1.0 / (1.0 + jnp.exp(-pre))
    grad = (out_grad[...].astype(F32) * (sig * (1.0 + pre * (1.0 - sig)))).astype(BF16)
    grads[c] = grad.T

    got = set()

    def have(kind, d):
        if (kind, d) not in got:
            got.add((kind, d))
            landed(grads.at[in_col(-d, 0 if kind == "z1" else 1)], g_r[kind].at[d % NZ])

    def second(d):
        return "z2" if d in GET_BOTH else "dg" if d in GET_CROSS else "x"

    def follow(plan):
        for kind, d in plan:
            p = d if kind == "x" else GET_PARENT[d]
            if kind == "z2":
                have(second(p), p)
            elif p != 0:
                have("z1", p)
            block = grads.at[in_col(-p, 1 if kind == "z2" else 0)]
            to = in_col(d - p, 1 if kind in ("x", "dg") else 0)
            send(block, block, g_s[kind].at[d % NZ], g_r[kind].at[d % NZ], r, to)

    follow(GET_FIRST)
    act_out[...] = (pre * sig).astype(BF16)
    wgrad = lax.dot_general(agg, grad, (((0,), (0,)), ((), ())), preferred_element_type=F32)
    bgrad = jnp.sum(grad.astype(F32).reshape(16, 8, SIDE), axis=0)
    ws[:, 0:8, :] = wgrad.reshape(N_ROW, 8, SIDE)
    ws[:, 8:16, :] = jnp.broadcast_to(bgrad[None], (N_ROW, 8, SIDE))
    for k, (dy, dx, dk) in enumerate(ROW_PEERS):
        to = in_row(dy, dx, dk)
        send(ws.at[to], wr.at[k], w_s.at[k], w_r.at[k], to, c)

    follow(GET_NEXT)
    total = ws[r]
    for k in range(len(ROW_PEERS)):
        landed(wr.at[k], w_r.at[k])
        total += wr[k]
    acc_a[...] = total
    for k, (dz, dh) in enumerate(ROUND_A):
        send(acc_a, wra.at[k], a_s.at[k], a_r.at[k], r, in_col(dz, dh))
    follow(GET_LAST)
    total = acc_a[...]
    for k in range(len(ROUND_A)):
        landed(wra.at[k], a_r.at[k])
        total += wra[k]
    acc_b[...] = total
    for k, (dz, dh) in enumerate(ROUND_B):
        send(acc_b, wrb.at[k], b_s.at[k], b_r.at[k], r, in_col(dz, dh))
    have("x", 0)
    for d in GET_PARENT:
        have("z1", d)
        have(second(d), d)

    def backward(t, carry):
        prod = jnp.dot(grads[tab[0, t]], tiles[t], preferred_element_type=F32)
        partial[t + 1] = prod + partial[tab[3, t]]
        return carry

    lax.fori_loop(0, SLOTS, backward, 0, unroll=True)

    for k, (dy, dx) in enumerate(CHIPS + ((0, 0),)):
        cs[k] = partial[tab[5, in_row(dy, dx, 1)]].astype(BF16)
        send(cs.at[k], cr.at[k], c_s.at[k], c_r.at[k], in_row(0, 0, 1), c)
    for k, (dy, dx) in enumerate(CHIPS):
        landed(cr.at[k], c_r.at[k])
        hs[k] = (partial[tab[5, in_row(dy, dx, 0)]] + cr[k].astype(F32)).astype(BF16)
        send(hs.at[k], hr.at[k], h_s.at[k], h_r.at[k], in_row(dy, dx, 0), c)

    total = acc_b[...]
    for k in range(len(ROUND_B)):
        landed(wrb.at[k], b_r.at[k])
        total += wrb[k]
    fin[r] = total[0:8]
    bg_out[...] = jnp.sum(total[8:16], axis=0, keepdims=True)
    for k, (dy, dx, dk) in enumerate(ROW_PEERS):
        send(fin.at[r], fin.at[r], e_s.at[k], e_r.at[k], in_row(dy, dx, dk), c)

    landed(cr.at[7], c_r.at[7])
    total = partial[tab[5, r]] + cr[7].astype(F32)
    for k in (6, 4, 5, 1, 2, 3, 0):
        landed(hr.at[k], h_r.at[k])
        total += hr[k].astype(F32)
    back_out[...] = total.astype(BF16)
    for k, (dy, dx, dk) in enumerate(ROW_PEERS):
        landed(fin.at[in_row(4 - dy, dx, dk)], e_r.at[k])
    wg_out[...] = fin[...].reshape(SIDE, SIDE)
    for copy in started:
        copy.wait_send()


def finish(act, back, weight, wg, bg, act_out, xg_out, wg_out, bg_out):
    act_out[...] = act[...]
    xg_out[...] = lax.dot_general(
        back[...], weight[...], (((0,), (1,)), ((), ())), preferred_element_type=F32
    ).astype(BF16)
    wg_out[...] = wg[...]
    bg_out[...] = bg[...]


def on_device(features, weight, bias, tile_values, tile_rows, tile_cols, tile_counts, out_grad):
    vmem = pl.BlockSpec(memory_space=pltpu.VMEM)
    dma = pltpu.SemaphoreType.DMA
    block = (SIDE, SIDE)
    hbm = pl.BlockSpec(memory_space=pltpu.HBM)
    act, back, wg, bg = pl.pallas_call(
        kernel,
        name="gcn",
        out_shape=(
            jax.ShapeDtypeStruct(block, BF16),
            jax.ShapeDtypeStruct(block, BF16),
            jax.ShapeDtypeStruct(block, F32),
            jax.ShapeDtypeStruct((1, SIDE), F32),
        ),
        in_specs=[hbm] * 8,
        out_specs=(vmem,) * 4,
        scratch_shapes=[
            pltpu.VMEM(block, BF16),
            pltpu.VMEM((1, SIDE), F32),
            pltpu.VMEM((1, SLOTS), jnp.int32),
            pltpu.VMEM((1, SLOTS), jnp.int32),
            pltpu.SMEM((1, 1), jnp.int32),
            pltpu.VMEM(block, BF16),
            pltpu.VMEM((SLOTS,) + block, BF16),
            pltpu.VMEM((N_ROW,) + block, BF16),
            pltpu.VMEM((SLOTS + 1,) + block, F32),
            pltpu.VMEM((N_COL,) + block, BF16),
            pltpu.VMEM((8, SIDE), jnp.int32),
            pltpu.SMEM((8, SIDE), jnp.int32),
            *[pltpu.VMEM((NZ,) + block, BF16)] * 6,
            pltpu.VMEM((8,) + block, BF16),
            pltpu.VMEM((8,) + block, BF16),
            pltpu.VMEM((7,) + block, BF16),
            pltpu.VMEM((7,) + block, BF16),
            pltpu.VMEM((N_ROW, 16, SIDE), F32),
            pltpu.VMEM((15, 16, SIDE), F32),
            pltpu.VMEM((16, SIDE), F32),
            pltpu.VMEM((3, 16, SIDE), F32),
            pltpu.VMEM((16, SIDE), F32),
            pltpu.VMEM((7, 16, SIDE), F32),
            pltpu.VMEM((N_ROW, 8, SIDE), F32),
            dma((9,)),
            pltpu.SemaphoreType.REGULAR,
            dma((8,)), dma((8,)), dma((7,)), dma((7,)),
            *[dma((NZ,))] * 14,
            dma((8,)), dma((8,)), dma((7,)), dma((7,)),
            dma((15,)), dma((15,)), dma((3,)), dma((3,)), dma((7,)), dma((7,)), dma((15,)), dma((15,)),
        ],
        compiler_params=pltpu.CompilerParams(
            collective_id=0, has_side_effects=True, vmem_limit_bytes=60 << 20
        ),
    )(
        features, weight, bias.reshape(1, SIDE), tile_values[0, 0],
        tile_rows[0], tile_cols[0], tile_counts, out_grad,
    )
    act, xg, wg, bg = pl.pallas_call(
        finish,
        name="finish",
        out_shape=(
            jax.ShapeDtypeStruct(block, BF16),
            jax.ShapeDtypeStruct(block, BF16),
            jax.ShapeDtypeStruct(block, F32),
            jax.ShapeDtypeStruct((1, SIDE), F32),
        ),
        in_specs=[vmem] * 5,
        out_specs=(vmem,) * 4,
    )(act, back, weight, wg, bg)
    return act, xg, wg, bg.reshape(SIDE)


def solution(mesh):
    return jax.shard_map(
        on_device,
        mesh=mesh,
        in_specs=(
            P(("row", "col"), None),
            P(),
            P(),
            P("row", "col", None, None, None),
            P("row", "col", None),
            P("row", "col", None),
            P("row", "col"),
            P(("row", "col"), None),
        ),
        out_specs=(P(("row", "col"), None), P(("row", "col"), None), P(), P()),
        check_vma=False,
    )
```

time: 85.6 us -> 72.3 us (0.84)
  local copies, waits for them, and re-layouts: 7.89 us -> 0 us
  Pallas kernels: 75.8 us -> 70.8 us
    unnamed x18 -> x0, local copies, waits for them, and re-layouts: 7.89 us -> none
    pallas_call x1, Pallas kernels: 75.8 us -> 69.1 us  [on_device(): pl.pallas_call(kernel, name='gcn', out_shape=(jax.ShapeDtypeStruct(block,...]
    pallas_call x0 -> x1, Pallas kernels: none -> 1.69 us  [on_device(): pl.pallas_call(finish, name='finish', out_shape=(jax.ShapeDtypeStruct(blo...]
where the time goes in v2:
time: 72.3 us; the launch traced here: 72.1 us
  Pallas kernels  70.8 us (98%)
  between operations  1.29 us (2%)
    pallas_call x1, Pallas kernels, on_device(): pl.pallas_call(kernel, name='gcn', out_shape=(jax.ShapeDtypeStruct(block,...  69.1 us
    pallas_call x1, Pallas kernels, on_device(): pl.pallas_call(finish, name='finish', out_shape=(jax.ShapeDtypeStruct(blo...  1.69 us

profile of v2, /device:TPU:1, one launch (start us, length us, event | category | flops | bytes accessed | tf_op | source)
XLA Modules:
  0.0 72.1 jit_solution(13706591959595275775)
XLA Ops:
  1.3 69.1 %gcn.1 = (bf16[128,128]{1,0:T(8,128)(2,1)}, bf16[128,128]{1,0:T(8,128)(2,1)}, f32[128,128]{1,0:T(8,128)}, f32[1,128]{1,0:T(1,128)}) custom-call(bf16[128,128]{1,0:T(8,128)(2,1)} %feat_hbm.1, bf16[128,128]{1,0:T(8,128)(2,1)} %weight.1, f32[1,128]{1,0:T(1,128)} %bitcast.6, bf16[38,128,128]{2,1,0:T(8,128)(2,1)} %bitcast.5, s32[1,38]{1,0:T(1,128)} %bitcast.7, ...), custom_call_target="tpu_custom_call" | custom-call | tf_op jit(solution)/shard_map/gcn/pallas_call | solution.py:289
  70.4 1.7 %finish.1 = (bf16[128,128]{1,0:T(8,128)(2,1)}, bf16[128,128]{1,0:T(8,128)(2,1)}, f32[128,128]{1,0:T(8,128)}, f32[1,128]{1,0:T(1,128)}) custom-call(bf16[128,128]{1,0:T(8,128)(2,1)} %get-tuple-element.12.act, bf16[128,128]{1,0:T(8,128)(2,1)} %get-tuple-element.13.back, bf16[128,128]{1,0:T(8,128)(2,1)} %weight.1, f32[128,128]{1,0:T(8,128)} %get-tuple-element.14.wg, ...), custom_call_target="tpu_custom_call" | custom-call | tf_op jit(solution)/shard_map/finish/pallas_call | solution.py:339

commit v3 on v2

--- a/solution.py
+++ b/solution.py
@@ -14,16 +14,10 @@
 N_ROW, N_COL = 16, 32
 
 CHIPS = ((2, 1), (2, 0), (1, 1), (3, 1), (1, 0), (3, 0), (0, 1))
-SUM_PARENT = {
-    -7: -6, -6: -5, -5: 0, -4: -5, -3: -2, -2: 0, -1: 0, 1: 0, 2: 0, 3: 2, 4: 5, 5: 0, 6: 5, 7: 6, 8: 5,
-}
-SUM_BOTH = (-7, -6, -3, 3, 6, 7)
-SUM_PLAN = (
-    ("z2", 7), ("x", 8), ("z2", -7), ("z1", -7), ("x", -4), ("z2", -3), ("z1", 7), ("x", 4), ("x", 0), ("x", 1),
-    ("z2", 3), ("x", -1), ("z1", -3), ("z1", 3), ("z2", 6), ("z2", -6), ("z1", 6), ("z1", -6), ("z1", 8), ("x", 2),
-    ("x", -2), ("z1", -4), ("z1", 4), ("x", 5), ("x", -5), ("z1", 1), ("z1", -1), ("z1", 2), ("z1", -2), ("z1", 5),
-    ("z1", -5),
-)
+SUM_PARENT = {-7: -6, -6: 0, -5: -6, -4: -3, -3: -1, -2: -1, -1: 0, 1: 0, 2: 3, 3: 1, 4: 3, 5: 6, 6: 0, 7: 6, 8: 6}
+SUM_BOTH = (-5, -4, 2, 3, 4, 5)
+SUM_CROSS = (-3, 7)
+SUM_PLAN = (('z2', -5), ('z2', 2), ('x', 8), ('z1', -4), ('z1', 4), ('z2', 5), ('x', -7), ('dg', 7), ('z2', 4), ('z1', 7), ('x', -2), ('z1', 5), ('z2', -4), ('z1', -5), ('z1', 2), ('x', 0), ('x', -1), ('x', -6), ('z1', 8), ('z1', -3), ('z1', -7), ('x', 6), ('z2', 3), ('z1', -2), ('dg', -3), ('z1', 3), ('z1', -6), ('z1', 6), ('x', 1), ('z1', -1), ('z1', 1))
 GET_PARENT = {
     -7: -6, -6: 0, -5: -6, -4: -3, -3: -2, -2: 0, -1: -2, 1: 2, 2: 0, 3: 2, 4: 3, 5: 6, 6: 0, 7: 6, 8: 7,
 }
@@ -44,10 +38,10 @@
 
 def kernel(
     feat_hbm, weight_hbm, bias_hbm, tiles_hbm, rows_hbm, cols_hbm, counts_hbm, out_grad_hbm,
-    act_out, back_out, wg_out, bg_out,
+    act_out, xg_out, wg_out, bg_out,
     weight, bias, rows, cols, counts, out_grad, tiles, panel, partial, grads, table, tab,
-    xs, xr, z1s, z1r, z2s, z2r, cs, cr, hs, hr, ws, wr, acc_a, wra, acc_b, wrb, fin,
-    sem, ring, p_s, p_r, f_s, f_r, xs_s, xs_r, z1_s, z1_r, z2_s, z2_r,
+    xs, xr, z1s, z1r, z2s, z2r, dgr, cs, cr, hs, hr, ws, wr, acc_a, wra, acc_b, wrb, fin,
+    sem, ring, p_s, p_r, f_s, f_r, xs_s, xs_r, z1_s, z1_r, z2_s, z2_r, dg_s, dg_r,
     g1_s, g1_r, g2_s, g2_r, gd_s, gd_r, gx_s, gx_r,
     c_s, c_r, h_s, h_r, w_s, w_r, a_s, a_r, b_s, b_r, e_s, e_r,
 ):
@@ -80,6 +74,13 @@
     started = []
     g_s = {"z1": g1_s, "z2": g2_s, "dg": gd_s, "x": gx_s}
     g_r = {"z1": g1_r, "z2": g2_r, "dg": gd_r, "x": gx_r}
+    barrier = pltpu.get_barrier_semaphore()
+    greet = [(in_row(dy, dx, 0), c) for dy, dx in CHIPS[:1]] + [(r, in_col(d, 0)) for d in (3, -3, 2, -2)]
+    greet += [(r, in_col(0, 1))] + [(in_row(dy, dx, 0), c) for dy, dx in CHIPS[1:]]
+    greet += [(r, in_col(d, 0)) for d in (1, -1)] + [(in_row(0, 0, 1), c)]
+    for row, col in greet:
+        pl.semaphore_signal(barrier, inc=1, device_id=(row, col), device_id_type=MESH)
+
     fetch = [
         pltpu.make_async_copy(src, dst, sem.at[k])
         for k, (src, dst) in enumerate(
@@ -92,12 +93,15 @@
     for copy in fetch:
         copy.start()
 
-    barrier = pltpu.get_barrier_semaphore()
-    greet = [(in_row(0, 0, 1), c)] + [(in_row(dy, dx, 0), c) for dy, dx in CHIPS]
-    greet += [(r, in_col(0, 1))] + [(r, in_col(d, 0)) for d in (1, -1, 2, -2, 3, -3)]
-    for row, col in greet:
-        pl.semaphore_signal(barrier, inc=1, device_id=(row, col), device_id_type=MESH)
-
+    fetch[0].wait()
+    pl.semaphore_wait(barrier, len(greet))
+
+    for dz, dh in ((3, 0), (-3, 0), (0, 1)):
+        pl.semaphore_signal(ring, inc=1, device_id=(r, in_col(dz, dh)), device_id_type=MESH)
+
+    for k, (dy, dx) in enumerate(CHIPS):
+        send(panel.at[r], panel.at[r], p_s.at[k], p_r.at[k], in_row(dy, dx, 0), c)
+    send(panel.at[r], panel.at[r], p_s.at[7], p_r.at[7], in_row(0, 0, 1), c)
     for k in (1, 2, 3):
         fetch[k].wait()
     lane = lax.broadcasted_iota(jnp.int32, (SIDE, SIDE), 1)
@@ -118,15 +122,7 @@
     to_scalar.start()
     partial[0] = jnp.zeros((SIDE, SIDE), F32)
 
-    fetch[0].wait()
-    pl.semaphore_wait(barrier, len(greet))
-
-    for d in (3, -3):
-        pl.semaphore_signal(ring, inc=1, device_id=(r, in_col(d, 0)), device_id_type=MESH)
-
-    for k, (dy, dx) in enumerate(CHIPS):
-        send(panel.at[r], panel.at[r], p_s.at[k], p_r.at[k], in_row(dy, dx, 0), c)
-    send(panel.at[r], panel.at[r], p_s.at[7], p_r.at[7], in_row(0, 0, 1), c)
+
     for k in (6, 4, 5, 1, 2, 3, 0):
         dy, dx = CHIPS[k]
         p = in_row(4 - dy, dx, 0)
@@ -145,7 +141,7 @@
 
     lax.fori_loop(0, SLOTS, forward, 0, unroll=True)
 
-    pl.semaphore_wait(ring, 2)
+    pl.semaphore_wait(ring, 3)
 
     def collect(e, kind):
         i = e % NZ
@@ -156,7 +152,10 @@
                 buf, got = (z1r, z1_r) if kind == "z1" else (z2r, z2_r)
                 landed(buf.at[q % NZ], got.at[q % NZ])
                 value += buf[q % NZ].astype(F32)
-        if kind == "z1" and e not in SUM_BOTH:
+            if SUM_PARENT[q] == e and kind == "z1" and q in SUM_CROSS:
+                landed(dgr.at[q % NZ], dg_r.at[q % NZ])
+                value += dgr[q % NZ].astype(F32)
+        if kind == "z1" and e not in SUM_BOTH + SUM_CROSS:
             landed(xr.at[i], xs_r.at[i])
             value += xr[i].astype(F32)
         return value
@@ -170,6 +169,9 @@
         elif kind == "z1":
             z1s[i] = value
             send(z1s.at[i], z1r.at[i], z1_s.at[i], z1_r.at[i], r, in_col(SUM_PARENT[e] - e, 0))
+        elif kind == "dg":
+            z2s[i] = value
+            send(z2s.at[i], dgr.at[i], dg_s.at[i], dg_r.at[i], r, in_col(SUM_PARENT[e] - e, 1))
         else:
             z2s[i] = value
             send(z2s.at[i], z2r.at[i], z2_s.at[i], z2_r.at[i], r, in_col(SUM_PARENT[e] - e, 0))
@@ -205,29 +207,29 @@
             send(block, block, g_s[kind].at[d % NZ], g_r[kind].at[d % NZ], r, to)
 
     follow(GET_FIRST)
-    act_out[...] = (pre * sig).astype(BF16)
     wgrad = lax.dot_general(agg, grad, (((0,), (0,)), ((), ())), preferred_element_type=F32)
     bgrad = jnp.sum(grad.astype(F32).reshape(16, 8, SIDE), axis=0)
-    ws[:, 0:8, :] = wgrad.reshape(N_ROW, 8, SIDE)
-    ws[:, 8:16, :] = jnp.broadcast_to(bgrad[None], (N_ROW, 8, SIDE))
+    own = [wgrad.reshape(N_ROW, 8, SIDE), jnp.broadcast_to(bgrad[None], (N_ROW, 8, SIDE))]
+    ws[...] = jnp.concatenate(own, axis=1).astype(BF16)
     for k, (dy, dx, dk) in enumerate(ROW_PEERS):
         to = in_row(dy, dx, dk)
         send(ws.at[to], wr.at[k], w_s.at[k], w_r.at[k], to, c)
 
+    act_out[...] = (pre * sig).astype(BF16)
     follow(GET_NEXT)
-    total = ws[r]
+    total = ws[r].astype(F32)
     for k in range(len(ROW_PEERS)):
         landed(wr.at[k], w_r.at[k])
-        total += wr[k]
-    acc_a[...] = total
+        total += wr[k].astype(F32)
+    acc_a[...] = total.astype(BF16)
     for k, (dz, dh) in enumerate(ROUND_A):
         send(acc_a, wra.at[k], a_s.at[k], a_r.at[k], r, in_col(dz, dh))
     follow(GET_LAST)
-    total = acc_a[...]
+    total = acc_a[...].astype(F32)
     for k in range(len(ROUND_A)):
         landed(wra.at[k], a_r.at[k])
-        total += wra[k]
-    acc_b[...] = total
+        total += wra[k].astype(F32)
+    acc_b[...] = total.astype(BF16)
     for k, (dz, dh) in enumerate(ROUND_B):
         send(acc_b, wrb.at[k], b_s.at[k], b_r.at[k], r, in_col(dz, dh))
     have("x", 0)
@@ -250,21 +252,26 @@
         hs[k] = (partial[tab[5, in_row(dy, dx, 0)]] + cr[k].astype(F32)).astype(BF16)
         send(hs.at[k], hr.at[k], h_s.at[k], h_r.at[k], in_row(dy, dx, 0), c)
 
-    total = acc_b[...]
+    total = acc_b[...].astype(F32)
     for k in range(len(ROUND_B)):
         landed(wrb.at[k], b_r.at[k])
-        total += wrb[k]
+        total += wrb[k].astype(F32)
     fin[r] = total[0:8]
     bg_out[...] = jnp.sum(total[8:16], axis=0, keepdims=True)
     for k, (dy, dx, dk) in enumerate(ROW_PEERS):
         send(fin.at[r], fin.at[r], e_s.at[k], e_r.at[k], in_row(dy, dx, dk), c)
 
+    for copy in started[:-22]:
+        copy.wait_send()
+    del started[:-22]
     landed(cr.at[7], c_r.at[7])
     total = partial[tab[5, r]] + cr[7].astype(F32)
     for k in (6, 4, 5, 1, 2, 3, 0):
         landed(hr.at[k], h_r.at[k])
         total += hr[k].astype(F32)
-    back_out[...] = total.astype(BF16)
+    xg_out[...] = lax.dot_general(
+        total.astype(BF16), weight[...], (((0,), (1,)), ((), ())), preferred_element_type=F32
+    ).astype(BF16)
     for k, (dy, dx, dk) in enumerate(ROW_PEERS):
         landed(fin.at[in_row(4 - dy, dx, dk)], e_r.at[k])
     wg_out[...] = fin[...].reshape(SIDE, SIDE)
@@ -272,13 +279,13 @@
         copy.wait_send()
 
 
-def finish(act, back, weight, wg, bg, act_out, xg_out, wg_out, bg_out):
-    act_out[...] = act[...]
-    xg_out[...] = lax.dot_general(
-        back[...], weight[...], (((0,), (1,)), ((), ())), preferred_element_type=F32
-    ).astype(BF16)
-    wg_out[...] = wg[...]
-    bg_out[...] = bg[...]
+def finish(*refs):
+    sem = refs[8]
+    copies = [pltpu.make_async_copy(refs[k], refs[4 + k], sem.at[k]) for k in range(4)]
+    for copy in copies:
+        copy.start()
+    for copy in copies:
+        copy.wait()
 
 
 def on_device(features, weight, bias, tile_values, tile_rows, tile_cols, tile_counts, out_grad):
@@ -286,7 +293,11 @@
     dma = pltpu.SemaphoreType.DMA
     block = (SIDE, SIDE)
     hbm = pl.BlockSpec(memory_space=pltpu.HBM)
-    act, back, wg, bg = pl.pallas_call(
+
+    def in_hbm(value):
+        return pltpu.with_memory_space_constraint(value, pltpu.HBM)
+
+    act, xg, wg, bg = pl.pallas_call(
         kernel,
         name="gcn",
         out_shape=(
@@ -310,31 +321,31 @@
             pltpu.VMEM((N_COL,) + block, BF16),
             pltpu.VMEM((8, SIDE), jnp.int32),
             pltpu.SMEM((8, SIDE), jnp.int32),
-            *[pltpu.VMEM((NZ,) + block, BF16)] * 6,
+            *[pltpu.VMEM((NZ,) + block, BF16)] * 7,
             pltpu.VMEM((8,) + block, BF16),
             pltpu.VMEM((8,) + block, BF16),
             pltpu.VMEM((7,) + block, BF16),
             pltpu.VMEM((7,) + block, BF16),
-            pltpu.VMEM((N_ROW, 16, SIDE), F32),
-            pltpu.VMEM((15, 16, SIDE), F32),
-            pltpu.VMEM((16, SIDE), F32),
-            pltpu.VMEM((3, 16, SIDE), F32),
-            pltpu.VMEM((16, SIDE), F32),
-            pltpu.VMEM((7, 16, SIDE), F32),
+            pltpu.VMEM((N_ROW, 16, SIDE), BF16),
+            pltpu.VMEM((15, 16, SIDE), BF16),
+            pltpu.VMEM((16, SIDE), BF16),
+            pltpu.VMEM((3, 16, SIDE), BF16),
+            pltpu.VMEM((16, SIDE), BF16),
+            pltpu.VMEM((7, 16, SIDE), BF16),
             pltpu.VMEM((N_ROW, 8, SIDE), F32),
             dma((9,)),
             pltpu.SemaphoreType.REGULAR,
             dma((8,)), dma((8,)), dma((7,)), dma((7,)),
-            *[dma((NZ,))] * 14,
+            *[dma((NZ,))] * 16,
             dma((8,)), dma((8,)), dma((7,)), dma((7,)),
             dma((15,)), dma((15,)), dma((3,)), dma((3,)), dma((7,)), dma((7,)), dma((15,)), dma((15,)),
         ],
         compiler_params=pltpu.CompilerParams(
-            collective_id=0, has_side_effects=True, vmem_limit_bytes=60 << 20
+            collective_id=0, has_side_effects=True, vmem_limit_bytes=32 << 20
         ),
     )(
-        features, weight, bias.reshape(1, SIDE), tile_values[0, 0],
-        tile_rows[0], tile_cols[0], tile_counts, out_grad,
+        *[in_hbm(v) for v in (features, weight, bias.reshape(1, SIDE), tile_values[0, 0], tile_rows[0], tile_cols[0])],
+        tile_counts, in_hbm(out_grad),
     )
     act, xg, wg, bg = pl.pallas_call(
         finish,
@@ -345,9 +356,11 @@
             jax.ShapeDtypeStruct(block, F32),
             jax.ShapeDtypeStruct((1, SIDE), F32),
         ),
-        in_specs=[vmem] * 5,
-        out_specs=(vmem,) * 4,
-    )(act, back, weight, wg, bg)
+        in_specs=[vmem] * 4,
+        out_specs=(hbm,) * 4,
+        scratch_shapes=[dma((4,))],
+        compiler_params=pltpu.CompilerParams(vmem_limit_bytes=4 << 20),
+    )(act, xg, wg, bg)
     return act, xg, wg, bg.reshape(SIDE)
 
 

time: 72.3 us -> 70.2 us (0.971)
  Pallas kernels: 70.8 us -> 68.8 us
    pallas_call x1, Pallas kernels: 1.69 us -> 0.69 us  [on_device(): pl.pallas_call(finish, name='finish', out_shape=(jax.ShapeDtypeStruct(blo...]
    pallas_call x1, Pallas kernels: 69.1 us -> 68.1 us  [on_device(): pl.pallas_call(kernel, name='gcn', out_shape=(jax.ShapeDtypeStruct(block,...]
where the time goes in v3:
time: 70.2 us; the launch traced here: 70.1 us
  Pallas kernels  68.8 us (98%)
  between operations  1.29 us (2%)
    pallas_call x1, Pallas kernels, on_device(): pl.pallas_call(kernel, name='gcn', out_shape=(jax.ShapeDtypeStruct(block,...  68.1 us

profile of v3, /device:TPU:1, one launch (start us, length us, event | category | flops | bytes accessed | tf_op | source)
XLA Modules:
  0.0 70.1 jit_solution(7531815416110747503)
XLA Ops:
  1.3 68.1 %gcn.1 = (bf16[128,128]{1,0:T(8,128)(2,1)S(1)}, bf16[128,128]{1,0:T(8,128)(2,1)S(1)}, f32[128,128]{1,0:T(8,128)S(1)}, f32[1,128]{1,0:T(1,128)S(1)}) custom-call(bf16[128,128]{1,0:T(8,128)(2,1)} %feat_hbm.1, bf16[128,128]{1,0:T(8,128)(2,1)} %weight_hbm.1, f32[1,128]{1,0:T(1,128)} %bitcast.6, bf16[38,128,128]{2,1,0:T(8,128)(2,1)} %bitcast.5, s32[1,38]{1,0:T(1,128)} %bitcast.7, ...), custom_call_target="tpu_custom_call" | custom-call | tf_op jit(solution)/shard_map/gcn/pallas_call | solution.py:300
  69.4 0.7 finish.1

commit v4 on v3

--- a/solution.py
+++ b/solution.py
@@ -31,9 +31,12 @@
     ("x", 6), ("z1", 7), ("dg", 5), ("z1", 5), ("z1", -7), ("x", -6), ("z1", -5), ("z2", 1), ("z1", 4), ("z1", -4),
     ("z2", 4), ("x", -1), ("dg", 8), ("z1", 8), ("z2", -4), ("x", -5), ("z2", 7), ("z2", -7),
 )
-ROUND_A = ((4, 0), (12, 0), (8, 0))
-ROUND_B = ((0, 1), (1, 0), (15, 0), (2, 0), (1, 1), (15, 1), (2, 1))
-ROW_PEERS = tuple((dy, dx, dk) for dy in range(4) for dx in range(2) for dk in range(2) if (dy, dx, dk) != (0, 0, 0))
+ROUND_A = ((8, 0), (4, 0), (12, 0))
+ROUND_B = ((2, 1), (1, 1), (15, 1), (2, 0), (0, 1), (1, 0), (15, 0))
+ROW_PEERS = (
+    (2, 1, 0), (2, 1, 1), (2, 0, 0), (2, 0, 1), (1, 1, 0), (3, 1, 0), (1, 1, 1), (3, 1, 1),
+    (1, 0, 0), (3, 0, 0), (1, 0, 1), (3, 0, 1), (0, 1, 0), (0, 1, 1), (0, 0, 1),
+)
 
 
 def kernel(

time: 70.2 us -> 70.1 us (level)
  no operation moved by 1% of the time
where the time goes in v4:
time: 70.1 us; the launch traced here: 69.9 us
  Pallas kernels  68.6 us (98%)
  between operations  1.29 us (2%)
    pallas_call x1, Pallas kernels, on_device(): pl.pallas_call(kernel, name='gcn', out_shape=(jax.ShapeDtypeStruct(block,...  67.9 us

profile of v4, /device:TPU:1, one launch (start us, length us, event | category | flops | bytes accessed | tf_op | source)
XLA Modules:
  0.0 69.9 jit_solution(839896940969825695)
XLA Ops:
  1.3 67.9 %gcn.1 = (bf16[128,128]{1,0:T(8,128)(2,1)S(1)}, bf16[128,128]{1,0:T(8,128)(2,1)S(1)}, f32[128,128]{1,0:T(8,128)S(1)}, f32[1,128]{1,0:T(1,128)S(1)}) custom-call(bf16[128,128]{1,0:T(8,128)(2,1)} %feat_hbm.1, bf16[128,128]{1,0:T(8,128)(2,1)} %weight_hbm.1, f32[1,128]{1,0:T(1,128)} %bitcast.6, bf16[38,128,128]{2,1,0:T(8,128)(2,1)} %bitcast.5, s32[1,38]{1,0:T(1,128)} %bitcast.7, ...), custom_call_target="tpu_custom_call" | custom-call | tf_op jit(solution)/shard_map/gcn/pallas_call | solution.py:303
  69.2 0.7 finish.1

commit v5 on v4

--- a/solution.py
+++ b/solution.py
@@ -14,10 +14,10 @@
 N_ROW, N_COL = 16, 32
 
 CHIPS = ((2, 1), (2, 0), (1, 1), (3, 1), (1, 0), (3, 0), (0, 1))
-SUM_PARENT = {-7: -6, -6: 0, -5: -6, -4: -3, -3: -1, -2: -1, -1: 0, 1: 0, 2: 3, 3: 1, 4: 3, 5: 6, 6: 0, 7: 6, 8: 6}
-SUM_BOTH = (-5, -4, 2, 3, 4, 5)
-SUM_CROSS = (-3, 7)
-SUM_PLAN = (('z2', -5), ('z2', 2), ('x', 8), ('z1', -4), ('z1', 4), ('z2', 5), ('x', -7), ('dg', 7), ('z2', 4), ('z1', 7), ('x', -2), ('z1', 5), ('z2', -4), ('z1', -5), ('z1', 2), ('x', 0), ('x', -1), ('x', -6), ('z1', 8), ('z1', -3), ('z1', -7), ('x', 6), ('z2', 3), ('z1', -2), ('dg', -3), ('z1', 3), ('z1', -6), ('z1', 6), ('x', 1), ('z1', -1), ('z1', 1))
+SUM_PARENT = {-7: -6, -6: -4, -5: -4, -4: 0, -3: -2, -2: -1, -1: 0, 1: 0, 2: 1, 3: 2, 4: 0, 5: 4, 6: 4, 7: 6, 8: 6}
+SUM_BOTH = (-7, -6, -3, -2, -1, 1, 2, 3, 7)
+SUM_CROSS = ()
+SUM_PLAN = (('x', 8), ('z2', -7), ('z2', -3), ('z1', -7), ('z2', 7), ('z2', 3), ('z1', 3), ('z1', 7), ('x', 5), ('x', -5), ('z1', -3), ('x', 4), ('z2', -6), ('z1', 8), ('x', 6), ('z2', -2), ('z2', 2), ('z1', -6), ('z1', 5), ('z1', 2), ('z1', -5), ('z1', -2), ('x', -4), ('z1', 6), ('z2', -1), ('z2', 1), ('z1', 1), ('z1', -1), ('z1', -4), ('z1', 4), ('x', 0))
 GET_PARENT = {
     -7: -6, -6: 0, -5: -6, -4: -3, -3: -2, -2: 0, -1: -2, 1: 2, 2: 0, 3: 2, 4: 3, 5: 6, 6: 0, 7: 6, 8: 7,
 }

time: 70.1 us -> 69.8 us (level)
  no operation moved by 1% of the time
where the time goes in v5:
time: 69.8 us; the launch traced here: 69.7 us
  Pallas kernels  68.4 us (98%)
  between operations  1.29 us (2%)
    pallas_call x1, Pallas kernels, on_device(): pl.pallas_call(kernel, name='gcn', out_shape=(jax.ShapeDtypeStruct(block,...  67.7 us

profile of v5, /device:TPU:1, one launch (start us, length us, event | category | flops | bytes accessed | tf_op | source)
XLA Modules:
  0.0 69.7 jit_solution(9606027441105175392)
XLA Ops:
  1.3 67.7 %gcn.1 = (bf16[128,128]{1,0:T(8,128)(2,1)S(1)}, bf16[128,128]{1,0:T(8,128)(2,1)S(1)}, f32[128,128]{1,0:T(8,128)S(1)}, f32[1,128]{1,0:T(1,128)S(1)}) custom-call(bf16[128,128]{1,0:T(8,128)(2,1)} %feat_hbm.1, bf16[128,128]{1,0:T(8,128)(2,1)} %weight_hbm.1, f32[1,128]{1,0:T(1,128)} %bitcast.6, bf16[38,128,128]{2,1,0:T(8,128)(2,1)} %bitcast.5, s32[1,38]{1,0:T(1,128)} %bitcast.7, ...), custom_call_target="tpu_custom_call" | custom-call | tf_op jit(solution)/shard_map/gcn/pallas_call | solution.py:303
  69.0 0.7 finish.1
